TPU v7x, 32 devices: a whole 2x2x4 slice. The times are simulated.
32 devices in a mesh: groups: 2 (over y), dom: 4 (over z), orient: 2 (over x), shell: 2 (over core).
Axes of the slice: x: 2, y: 2, z: 4, core: 2. Of those that a mesh axis runs over, the one named last changes fastest.
Arguments:
- tiles: bfloat16 [64, 128, 128], P(('groups', 'dom')), parts along dimension 0, may hold values from -6 to 6
- particle_tile: int32 [512], P('groups'), parts along dimension 0, may hold values from 0 to 31, as said below
- particle_offset: int32 [512, 2], P('groups'), parts along dimension 0, may hold values from 0 to 32
- wedge_slope: int32 [32], P('groups'), parts along dimension 0, may hold values from 60 to 240
- rot_ref: bfloat16 [384, 18432], P(('groups', 'orient'), ('dom', 'shell')), parts along dimension 0, may hold values from -160 to 160
Outputs:
- new_reference: float32 [384, 18432], P(('groups', 'orient'), ('dom', 'shell')), parts along dimension 0
- particle_logz: float32 [512], P(('groups', 'dom')), parts along dimension 0
There are 2 independent parts, one for each index of `groups`. A program takes and returns all parts, laid end to end along the dimension named above; each array names one. Nothing has to cross between parts.
Inputs may be any that keep to these rules, and one draw needn't show every extreme that they name: `particle_tile`: each aligned block of 64 particles holds at most 32 particles whose tiles lie in one range k * 8 to (k + 1) * 8 - 1, and exactly 32 for some such range in every block.
All inputs are finite; a program needn't handle non-finite values.
Results may differ from a plain program's by a relative error of at most 0.0015.
The roundings to bfloat16 on the way count: a program that leaves them out, or rounds other values in their place, can miss the bound.
Values may be sent and summed in bfloat16 or wider, within the bound.
A program may use at most 64 MiB of HBM per device.

v0:
```python
import math

import jax
import jax.numpy as jnp
from jax import lax
from jax.sharding import PartitionSpec as P

BOX = 96
TOMOS = 16


def box_tables(kx_rows, box_width):
    positions = jnp.arange(box_width, dtype=jnp.int32)
    angle_step = 2.0 * math.pi / box_width
    phase_x = (kx_rows[:, None] * positions[None, :] % box_width).astype(jnp.float32) * angle_step
    phase_y = (positions[:, None] * positions[None, :] % box_width).astype(jnp.float32) * angle_step
    return (jnp.cos(phase_x), jnp.sin(phase_x), jnp.cos(phase_y), jnp.sin(phase_y))


def transform(boxes, tables, box_width):
    cos_x, sin_x, cos_y, sin_y = tables
    highest = lax.Precision.HIGHEST
    values = boxes.astype(jnp.float32)
    real_y = jnp.einsum("pyx,kx->pyk", values, cos_x, precision=highest)
    imag_y = -jnp.einsum("pyx,kx->pyk", values, sin_x, precision=highest)
    real_f = jnp.einsum("qy,pyk->pkq", cos_y, real_y, precision=highest) + jnp.einsum(
        "qy,pyk->pkq", sin_y, imag_y, precision=highest
    )
    imag_f = jnp.einsum("qy,pyk->pkq", cos_y, imag_y, precision=highest) - jnp.einsum(
        "qy,pyk->pkq", sin_y, real_y, precision=highest
    )
    spectrum = jnp.stack([real_f, imag_f], axis=2) * (1.0 / box_width)
    return spectrum.reshape(boxes.shape[0], -1).astype(jnp.bfloat16)


def wedge_grid(wedge_slope, kx_rows, box_width):
    freq_y = jnp.arange(box_width, dtype=jnp.int32)
    along_y = jnp.minimum(freq_y, box_width - freq_y)
    along_x = jnp.minimum(kx_rows, box_width - kx_rows)
    inside = along_y[None, None, :] * 100 <= wedge_slope[:, None, None] * along_x[None, :, None]
    grid = jnp.broadcast_to(
        inside[:, :, None, :], (wedge_slope.shape[0], kx_rows.shape[0], 2, box_width)
    )
    return grid.reshape(wedge_slope.shape[0], -1).astype(jnp.float32)


def local(tiles, particle_tile, particle_offset, wedge_slope, rot_ref):
    dom_count = lax.axis_size("dom")
    dom_index = lax.axis_index("dom")
    shell_count = lax.axis_size("shell")
    shell_index = lax.axis_index("shell")
    tile_dev = tiles.shape[0]
    tile_side = tiles.shape[1]
    part_dev = particle_tile.shape[0] // dom_count
    slot_count = 2 * part_dev // dom_count
    dom_rows = BOX // dom_count
    sub_rows = dom_rows // shell_count
    owners = jnp.arange(dom_count, dtype=jnp.int32)
    source_grid = (particle_tile // tile_dev).reshape(dom_count, part_dev)
    owner_hot = (source_grid[:, :, None] == owners[None, None, :]).astype(jnp.int32)
    slot_rank = jnp.sum(owner_hot * (jnp.cumsum(owner_hot, axis=1) - 1), axis=2)
    slot_ids = jnp.arange(slot_count, dtype=jnp.int32)
    matched = (
        (source_grid == dom_index)[:, :, None] & (slot_rank[:, :, None] == slot_ids[None, None, :])
    ).astype(jnp.int32)
    filled = jnp.sum(matched, axis=1).reshape(-1)
    row_in_block = jnp.sum(matched * jnp.arange(part_dev, dtype=jnp.int32)[None, :, None], axis=1)
    sender_ids = (owners[:, None] * part_dev + row_in_block).reshape(-1)
    tile_rows = particle_tile[sender_ids] - dom_index * tile_dev
    offsets = particle_offset[sender_ids]
    tile_pick = (
        (tile_rows[:, None] == jnp.arange(tile_dev, dtype=jnp.int32)[None, :])
        & (filled[:, None] > 0)
    ).astype(jnp.bfloat16)
    picked = jnp.dot(
        tile_pick, tiles.reshape(tile_dev, -1), preferred_element_type=jnp.float32
    ).astype(jnp.bfloat16)
    picked = picked.reshape(-1, tile_side, tile_side)
    box_pos = jnp.arange(BOX, dtype=jnp.int32)
    tile_pos = jnp.arange(tile_side, dtype=jnp.int32)
    row_select = (
        (offsets[:, 0][:, None] + box_pos[None, :])[:, :, None] == tile_pos[None, None, :]
    ).astype(jnp.bfloat16)
    col_select = (
        (offsets[:, 1][:, None] + box_pos[None, :])[:, :, None] == tile_pos[None, None, :]
    ).astype(jnp.bfloat16)
    row_cut = jnp.einsum(
        "byr,brc->byc", row_select, picked, preferred_element_type=jnp.float32
    ).astype(jnp.bfloat16)
    outgoing = jnp.einsum(
        "byc,bxc->byx", row_cut, col_select, preferred_element_type=jnp.float32
    ).astype(jnp.bfloat16)
    outgoing = outgoing.reshape(dom_count, slot_count, BOX, BOX)
    incoming = lax.all_to_all(outgoing, "dom", split_axis=0, concat_axis=0, tiled=True)
    own_source = lax.dynamic_index_in_dim(source_grid, dom_index, 0, keepdims=False)
    own_rank = lax.dynamic_index_in_dim(slot_rank, dom_index, 0, keepdims=False)
    slot_target = own_source * slot_count + own_rank
    slot_hot = (
        slot_target[:, None] == jnp.arange(dom_count * slot_count, dtype=jnp.int32)[None, :]
    ).astype(jnp.bfloat16)
    boxes = jnp.dot(
        slot_hot,
        incoming.reshape(dom_count * slot_count, BOX * BOX),
        preferred_element_type=jnp.float32,
    ).astype(jnp.bfloat16)
    boxes = boxes.reshape(part_dev, BOX, BOX)
    kx_shell = (
        owners[:, None] * dom_rows
        + shell_index * sub_rows
        + jnp.arange(sub_rows, dtype=jnp.int32)[None, :]
    ).reshape(-1)
    tables = box_tables(kx_shell, BOX)
    block_size = min(32, part_dev)
    spectra = lax.map(
        lambda group_boxes: transform(group_boxes, tables, BOX),
        boxes.reshape(part_dev // block_size, block_size, BOX, BOX),
    )
    spectra = spectra.reshape(part_dev, -1)
    tomograms = lax.dynamic_slice_in_dim(particle_tile, dom_index * part_dev, part_dev) % TOMOS
    tomo_hot = (tomograms[:, None] == jnp.arange(TOMOS, dtype=jnp.int32)[None, :]).astype(
        jnp.bfloat16
    )
    wedge_shell = wedge_grid(wedge_slope, kx_shell, BOX).astype(jnp.bfloat16)
    kept_mask = jnp.dot(tomo_hot, wedge_shell, preferred_element_type=jnp.bfloat16)
    weighted = spectra * kept_mask
    partial_scores = lax.dot_general(
        weighted,
        lax.all_gather(rot_ref, "dom", axis=1, tiled=True),
        (((1,), (1,)), ((), ())),
        preferred_element_type=jnp.float32,
    )
    scores = lax.psum(partial_scores, "shell") * (6.0 / BOX)
    row_top = lax.pmax(jnp.max(scores, axis=1), "orient")
    shifted = jnp.exp(scores - row_top[:, None])
    row_total = lax.psum(jnp.sum(shifted, axis=1), "orient")
    particle_logz = row_top + jnp.log(row_total)
    weights = (shifted / row_total[:, None]).astype(jnp.bfloat16)
    kx_mine = dom_index * dom_rows + shell_index * sub_rows + jnp.arange(sub_rows, dtype=jnp.int32)
    wedge_mine = wedge_grid(wedge_slope, kx_mine, BOX)
    numerator = lax.psum_scatter(
        lax.dot_general(
            weighted, weights, (((0,), (0,)), ((), ())), preferred_element_type=jnp.float32
        ),
        "dom",
        scatter_dimension=0,
        tiled=True,
    ).T
    tomo_weight = lax.psum(jnp.dot(tomo_hot.T, weights, preferred_element_type=jnp.float32), "dom")
    denominator = jnp.dot(
        tomo_weight.T,
        wedge_mine,
        precision=lax.Precision.HIGHEST,
        preferred_element_type=jnp.float32,
    )
    return (numerator / (denominator + 1.0), particle_logz)


def solution(mesh):
    in_specs = (
        P(("groups", "dom"), None, None),
        P("groups"),
        P("groups", None),
        P("groups"),
        P(("groups", "orient"), ("dom", "shell")),
    )
    out_specs = (P(("groups", "orient"), ("dom", "shell")), P(("groups", "dom")))
    return jax.shard_map(local, mesh=mesh, in_specs=in_specs, out_specs=out_specs, check_vma=False)
```

profile of v0, /device:TPU:0, one launch (start us, length us, event | category | flops | bytes accessed | tf_op | source)
XLA Modules:
  0.0 255.1 jit_solution(16030934890638751260)
XLA Ops:
  8.9 1.6 gather_fusion.1
  10.6 2.2 fusion.91
  12.8 3.2 %copy.13 = bf16[16,8,128,128]{3,2,1,0:T(8,128)(2,1)} copy(bf16[16,8,128,128]{3,1,2,0:T(8,128)(2,1)S(1)} %fusion.91) | data formatting | bytes 8388608
  17.1 7.1 %fusion.88 = bf16[128,96,96]{2,1,0:T(8,128)(2,1)} fusion(s32[128,96]{1,0:T(8,128)S(1)} %get-tuple-element.111, bf16[128,128,128]{2,1,0:T(8,128)(2,1)} %bitcast.84, s32[128,96]{1,0:T(8,128)S(1)} %get-tuple-element.112), kind=kOutput, calls=%fused_computation.89 | convolution fusion | flops 710541312 | bytes 6651904 | tf_op jit(solution)/shard_map/byc,bxc->byx/dot_general | solution.py:90
  24.2 6.5 %all-to-all-start = ((bf16[4,32,96,96]{3,2,1,0:T(8,128)(2,1)}), bf16[4,32,96,96]{3,2,1,0:T(8,128)(2,1)S(1)}, u32[]{:S(2)}, u32[]{:S(2)}) async-start(bf16[4,32,96,96]{3,2,1,0:T(8,128)(2,1)} %bitcast.85), calls=%async_computation | async-start | bytes 6291456 | tf_op jit(solution)/shard_map/all_to_all | solution.py:94
  32.7 1.2 convert_element_type.75
  34.1 95.7 %all-to-all-done = bf16[4,32,96,96]{3,2,1,0:T(8,128)(2,1)S(1)} async-done(((bf16[4,32,96,96]{3,2,1,0:T(8,128)(2,1)}), bf16[4,32,96,96]{3,2,1,0:T(8,128)(2,1)S(1)}, u32[]{:S(2)}, u32[]{:S(2)}) %all-to-all-start) | async-done | bytes 2359328 | tf_op jit(solution)/shard_map/all_to_all | solution.py:94
  129.8 5.1 %reshape.280 = bf16[128,9216]{1,0:T(8,128)(2,1)} reshape(bf16[4,32,96,96]{3,2,1,0:T(8,128)(2,1)S(1)} %all-to-all-done) | data formatting | bytes 4718592 | tf_op jit(solution)/shard_map/reshape | solution.py:103
  134.8 2.2 convolution_convert_fusion.1
  137.0 1.6 reshape_reshape.3
  138.6 21.0 %while.13 = (s32[]{:T(128)}, bf16[2,32,9216]{2,1,0:T(8,128)(2,1)}, bf16[2,32,96,96]{3,2,1,0:T(8,128)(2,1)S(1)}, s32[48]{0:T(128)S(1)}, s32[]{:T(128)}) while((s32[]{:T(128)}, bf16[2,32,9216]{2,1,0:T(8,128)(2,1)}, bf16[2,32,96,96]{3,2,1,0:T(8,128)(2,1)S(1)}, s32[48]{0:T(128)S(1)}, s32[]{:T(128)}) %tuple.34), condition=%wide.region_5.6_spmd.clone.clone.clone, body=%wide.region_4.5_spmd.clone.clone.clone.sunk | while | flops 1020957696 | bytes 13960773 | solution.py:114
  138.6 1.8 convolution_negate_fusion.2
  141.4 1.8 fusion.155
  143.2 1.0 fusion.156
  145.2 1.0 fusion.158
  147.2 1.1 convert_element_type.161
  149.1 1.8 convolution_negate_fusion.2
  150.9 1.0 fusion.154
  151.9 1.8 fusion.155
  153.7 1.0 fusion.156
  154.7 1.0 fusion.157
  155.6 1.0 fusion.158
  157.7 1.1 convert_element_type.161
  159.6 1.8 convolution_multiply_fusion
  161.4 2.2 fusion.108
  163.7 3.4 %psum.21 = f32[64,96]{1,0:T(8,128)S(1)} all-reduce(f32[64,96]{1,0:T(8,128)S(1)} %fusion.108), channel_id=1, replica_groups=mesh['groups'=2,'dom'=4,'orient'=2,'shell'=2] {'shell'}, use_global_device_ids=true, to_apply=%region_6.7 | all-reduce | flops 6144 | bytes 49152 | tf_op jit(solution)/shard_map/psum | solution.py:132
  167.2 4.9 %pmax.7 = f32[64]{0:T(128)S(1)} all-reduce(f32[64]{0:T(128)S(1)} %multiply_reduce_fusion), channel_id=1, replica_groups=mesh['groups'=2,'dom'=4,'orient'=2,'shell'=2] {'orient'}, use_global_device_ids=true, to_apply=%region_8.9 | all-reduce | flops 64 | bytes 512 | tf_op jit(solution)/shard_map/pmax | solution.py:133
  172.3 4.9 %psum.22 = f32[64]{0:T(128)S(1)} all-reduce(f32[64]{0:T(128)S(1)} %fusion.101), channel_id=1, replica_groups=mesh['groups'=2,'dom'=4,'orient'=2,'shell'=2] {'orient'}, use_global_device_ids=true, to_apply=%region_10.11 | all-reduce | flops 64 | bytes 512 | tf_op jit(solution)/shard_map/psum | solution.py:135
  177.3 2.4 fusion.109
  181.1 10.5 %psum.23 = f32[16,96]{1,0:T(8,128)S(1)} all-reduce(f32[16,96]{1,0:T(8,128)S(1)} %fusion.98), channel_id=1, replica_groups=mesh['groups'=2,'dom'=4,'orient'=2,'shell'=2] {'dom'}, use_global_device_ids=true, to_apply=%region_12.13 | all-reduce | flops 1536 | bytes 12288 | tf_op jit(solution)/shard_map/psum | solution.py:148
  192.1 53.5 %reduce-scatter.2.cloned.1.call-done = f32[2304,96]{0,1:T(8,128)} async-done(((f32[9216,96]{0,1:T(8,128)}), f32[2304,96]{0,1:T(8,128)}) %reduce-scatter.2.cloned.1.call-update) | async-done | bytes 884752 | tf_op jit(solution)/shard_map/reduce_scatter | solution.py:140
  245.6 2.7 %fusion.84 = f32[96,2304]{1,0:T(8,128)} fusion(f32[16,96]{1,0:T(8,128)S(1)} %psum.23, pred[16,2304]{1,0:T(8,128)(4,1)S(1)} %reshape.282, f32[2304,96]{0,1:T(8,128)} %reduce-scatter.2.cloned.1.call-done), kind=kOutput, calls=%fused_computation.85 | convolution fusion | flops 42909696 | bytes 1812480 | tf_op jit(solution)/shard_map/dot_general | solution.py:149
  (67 shorter events, 12.9 us)
Async XLA Ops:
  12.8 3.2 %copy-start.2 = (s32[256,2]{0,1:T(2,128)S(1)}, s32[256,2]{0,1:T(2,128)}, u32[]{:S(2)}) copy-start(s32[256,2]{0,1:T(2,128)} %param.9) | copy-start | bytes 6148
  24.2 7.6 %copy-start.3 = (s32[16]{0:T(128)S(1)}, s32[16]{0:T(128)}, u32[]{:S(2)}) copy-start(s32[16]{0:T(128)} %param.10) | copy-start | bytes 196
  24.2 105.6 %all-to-all-start = ((bf16[4,32,96,96]{3,2,1,0:T(8,128)(2,1)}), bf16[4,32,96,96]{3,2,1,0:T(8,128)(2,1)S(1)}, u32[]{:S(2)}, u32[]{:S(2)}) async-start(bf16[4,32,96,96]{3,2,1,0:T(8,128)(2,1)} %bitcast.85), calls=%async_computation | async-start | bytes 6291456 | tf_op jit(solution)/shard_map/all_to_all | solution.py:94
  30.6 3.3 %copy-start = (s32[256]{0:T(256)S(1)}, s32[256]{0:T(256)}, u32[]{:S(2)}) copy-start(s32[256]{0:T(256)} %param.8) | copy-start | bytes 3076
  30.6 130.8 %all-gather.2.cloned.1.call-start = ((), (), s32[]{:S(2)}) async-start(), calls=%async_computation.2 | async-start | bytes 2211840 | tf_op jit(solution)/shard_map/all_gather | solution.py:128
  31.4 214.2 %reduce-scatter.2.cloned.1.call-start = ((), (), s32[]{:S(2)}) async-start(), calls=%async_computation.3 | async-start | bytes 4423680 | tf_op jit(solution)/shard_map/reduce_scatter | solution.py:140
  31.8 0.6 copy-start.5
  138.6 21.0 %copy-start.1 = (bf16[16,9216]{1,0:T(8,128)(2,1)S(1)}, bf16[16,9216]{1,0:T(8,128)(2,1)}, u32[]{:S(2)}) copy-start(bf16[16,9216]{1,0:T(8,128)(2,1)} %convert_element_type.75) | copy-start | bytes 884740
  179.8 0.7 copy-start.4
  179.8 0.7 copy-start.6
Sparse Core Ops, SparseCore 0:
  33.0 66.7 all-gather.1
  179.9 65.6 reduce-scatter.1
where the time goes:
time: 256 us; the launch traced here: 255 us
  waiting for transfers between devices  150 us (59%)
  matrix products  35.8 us (14%)
  blocking collectives  23.8 us (9%)
  local copies, waits for them, and re-layouts  21 us (8%)
  between operations  14.3 us (6%)
  starting transfers between devices  6.67 us (3%)
  other arithmetic  3.5 us (1%)
    all_to_all x1, waiting for transfers between devices, local(): lax.all_to_all(outgoing, 'dom', split_axis=0, concat_axis=0, tiled=True)  95.7 us
    reduce_scatter x1, waiting for transfers between devices, local(): lax.psum_scatter(lax.dot_general(weighted, weights, (((0,), (0,)), ((), (...  53.5 us
    psum x1, blocking collectives, local(): lax.psum(jnp.dot(tomo_hot.T, weights, preferred_element_type=jnp.float32)...  10.5 us
    dot_general x1, matrix products, local(): jnp.einsum('byc,bxc->byx', row_cut, col_select, preferred_element_type=jn...  7.08 us
    all_to_all x1, starting transfers between devices, local(): lax.all_to_all(outgoing, 'dom', split_axis=0, concat_axis=0, tiled=True)  6.45 us
  transfers between devices with their start and end apart: 3, of which 2 were waited for; matrix products, arithmetic and copies ran while one was open for 14% of the time, Pallas kernels for 0%

commit v1 on v0

v1 whole, which is shorter than its diff:
```python
import functools
import math

import jax
import jax.numpy as jnp
import numpy as np
from jax import lax
from jax.experimental import pallas as pl
from jax.experimental.pallas import tpu as pltpu
from jax.sharding import PartitionSpec as P

BOX = 96
TOMOS = 16
LANES = 128
MESH = pl.DeviceIdType.MESH
VMEM = pl.BlockSpec(memory_space=pltpu.VMEM)
SMEM = pl.BlockSpec(memory_space=pltpu.SMEM)
ANY = pl.BlockSpec(memory_space=pl.ANY)
F32 = jnp.float32
BF16 = jnp.bfloat16
LIMIT = 56 * 1024 * 1024


def round_up(value, step):
    return -(-value // step) * step


def place(name, axis):
    return {name: axis}


def greet(peers):
    barrier = pltpu.get_barrier_semaphore()
    for peer in peers:
        pl.semaphore_signal(barrier, inc=1, device_id=peer, device_id_type=MESH)
    pl.semaphore_wait(barrier, len(peers))


def gather_kernel(
    doms, orients, shells, mine_ref, all_ref, own_sem, z_send, z_recv, x_send, x_recv, c_send, c_recv
):
    dom = lax.axis_index("dom")
    orient = lax.axis_index("orient")
    shell = lax.axis_index("shell")
    rows = mine_ref.shape[0]
    piece = rows // (orients * shells)
    z_peers = [lax.rem(dom + r, doms) for r in range(1, doms)]
    x_peers = [lax.rem(orient + r, orients) for r in range(1, orients)]
    c_peers = [lax.rem(shell + r, shells) for r in range(1, shells)]
    greet(
        [{"dom": z} for z in z_peers]
        + [{"orient": x} for x in x_peers]
        + [{"shell": c} for c in c_peers]
    )

    def part(block, x, c):
        start = pl.multiple_of(block * rows + (x * shells + c) * piece, 16)
        return all_ref.at[pl.ds(start, piece)]

    own = pltpu.make_async_copy(
        mine_ref, all_ref.at[pl.ds(pl.multiple_of(dom * rows, 16), rows)], own_sem
    )
    own.start()
    first = pl.multiple_of((orient * shells + shell) * piece, 16)
    started = []

    def send(source, target, send_sem, recv_sem, device):
        copy = pltpu.make_async_remote_copy(
            src_ref=source,
            dst_ref=target,
            send_sem=send_sem,
            recv_sem=recv_sem,
            device_id=device,
            device_id_type=MESH,
        )
        copy.start()
        started.append(copy)

    def arrived(target, send_sem, recv_sem, device):
        pltpu.make_async_remote_copy(
            src_ref=target,
            dst_ref=target,
            send_sem=send_sem,
            recv_sem=recv_sem,
            device_id=device,
            device_id_type=MESH,
        ).wait_recv()

    for r, z in enumerate(z_peers):
        send(
            mine_ref.at[pl.ds(first, piece)],
            part(dom, orient, shell),
            z_send.at[r],
            z_recv.at[dom],
            {"dom": z},
        )
    for r, z in enumerate(z_peers):
        held = part(z, orient, shell)
        arrived(held, z_send.at[r], z_recv.at[z], {"dom": z})
        for i, x in enumerate(x_peers):
            send(held, held, x_send.at[r, i], x_recv.at[z, orient], {"orient": x})
        for i, c in enumerate(c_peers):
            send(held, held, c_send.at[r, 0, i], c_recv.at[z, orient, shell], {"shell": c})
    for r, z in enumerate(z_peers):
        for k, x in enumerate(x_peers):
            held = part(z, x, shell)
            arrived(held, x_send.at[r, k], x_recv.at[z, x], {"orient": x})
            for i, c in enumerate(c_peers):
                send(held, held, c_send.at[r, 1 + k, i], c_recv.at[z, x, shell], {"shell": c})
    for r, z in enumerate(z_peers):
        for k in range(orients):
            x = lax.rem(orient + k, orients)
            for i, c in enumerate(c_peers):
                arrived(part(z, x, c), c_send.at[r, k, i], c_recv.at[z, x, c], {"shell": c})
    own.wait()
    for copy in started:
        copy.wait_send()


def gather_tiles(mine, doms, orients, shells):
    dma = pltpu.SemaphoreType.DMA
    return pl.pallas_call(
        functools.partial(gather_kernel, doms, orients, shells),
        out_shape=jax.ShapeDtypeStruct((doms * mine.shape[0], mine.shape[1]), mine.dtype),
        in_specs=[ANY],
        out_specs=ANY,
        scratch_shapes=[
            dma,
            dma((doms,)),
            dma((doms,)),
            dma((doms, orients)),
            dma((doms, orients)),
            dma((doms, orients, shells)),
            dma((doms, orients, shells)),
        ],
        compiler_params=pltpu.CompilerParams(collective_id=0, has_side_effects=True),
        name="gather_tiles",
    )(mine)


def split(values):
    high = values.astype(BF16)
    return high, (values - high.astype(F32)).astype(BF16)


def grid_rows(kx_first, width):
    lane = lax.broadcasted_iota(jnp.int32, (1, width), 1)
    kx_step = jnp.zeros_like(lane)
    ky = lane
    for edge in range(BOX, width, BOX):
        over = (lane >= edge).astype(jnp.int32)
        ky = ky - BOX * over
        if edge % (2 * BOX) == 0:
            kx_step = kx_step + over
    kx = kx_first + kx_step
    along_y = jnp.minimum(ky, BOX - ky) * 100
    along_x = jnp.minimum(kx, BOX - kx)
    return along_y.astype(F32), along_x.astype(F32)


def spectra_kernel(
    sub_rows,
    shells,
    code_ref,
    slope_ref,
    tiles_ref,
    x_ref,
    y_ref,
    rot_ref,
    weighted_ref,
    scores_ref,
    hot_ref,
    tile_t,
    x_tab,
    held,
    slopes,
    tomos,
):
    position = lax.axis_index("dom") * shells + lax.axis_index("shell")
    rows = x_ref.shape[1]
    particles = slopes.shape[0]
    base = x_ref[position]
    for shift in range(x_tab.shape[0]):
        moved = base if shift == 0 else pltpu.roll(base, shift, 1)
        high = moved.astype(BF16).astype(F32)
        x_tab[shift] = jnp.concatenate([high, moved - high], axis=0).astype(BF16)

    @pl.loop(0, tiles_ref.shape[0])
    def _(tile):
        tile_t[tile] = tiles_ref[tile].astype(F32).T.astype(BF16)

    unroll = 8

    @pl.loop(0, particles // unroll)
    def _(step):
        for part in range(unroll):
            particle = step * unroll + part
            code = code_ref[particle]
            tile = code >> 12
            start_y = (code >> 6) & 63
            start_x = code & 63
            both = jnp.dot(x_tab[start_x], tile_t[tile], preferred_element_type=F32)
            along = both[:rows] + both[rows:]
            along = pltpu.roll(along, (LANES - start_y) & (LANES - 1), 1)
            held[pl.ds(pl.multiple_of(particle * rows, 8), rows), :] = along
            tomo = lax.rem(tile, TOMOS)
            slope = slope_ref[tomo].astype(F32)
            slopes[pl.ds(particle, 1), :] = jnp.full((1, LANES), slope, F32)
            tomos[pl.ds(particle, 1), :] = jnp.full((1, LANES), tomo, jnp.int32)

    lane = lax.broadcasted_iota(jnp.int32, tomos.shape, 1)
    hot_ref[...] = jnp.where(tomos[...] == lane, 1.0, 0.0).astype(BF16)
    kx_first = position * sub_rows
    chunk = 256

    @pl.loop(0, particles // chunk)
    def _(block):
        first = pl.multiple_of(block * chunk, chunk)
        own_slope = slopes[pl.ds(first, chunk), :][:, :1]

        def lines(row, side):
            real = held[pl.ds(first * rows + row, chunk, stride=rows), :]
            imag = held[pl.ds(first * rows + sub_rows + row, chunk, stride=rows), :]
            high, low = split(jnp.concatenate([real, imag], axis=1))
            return (
                jnp.dot(high, y_ref[side, 0], preferred_element_type=F32)
                + jnp.dot(high, y_ref[side, 1], preferred_element_type=F32)
                + jnp.dot(low, y_ref[side, 0], preferred_element_type=F32)
            )

        for row in range(0, sub_rows, 2):
            even = lines(row, 0)
            if row + 1 < sub_rows:
                odd = lines(row + 1, 1)
                values = jnp.concatenate(
                    [even[:, :LANES], even[:, LANES:] + odd[:, :LANES], odd[:, LANES:]], axis=1
                )
            else:
                values = even[:, : 2 * BOX]
            width = values.shape[1]
            along_y, along_x = grid_rows(kx_first + row, width)
            inside = along_y <= own_slope * along_x
            values = jnp.where(inside, values * (1.0 / BOX), 0.0)
            weighted_ref[pl.ds(first, chunk), row * 2 * BOX : row * 2 * BOX + width] = values.astype(
                BF16
            )
        scores = lax.dot_general(
            weighted_ref[pl.ds(first, chunk), :],
            rot_ref[...],
            (((1,), (1,)), ((), ())),
            preferred_element_type=F32,
        )
        pad = scores_ref.shape[1] - scores.shape[1]
        scores_ref[pl.ds(first, chunk), :] = jnp.concatenate(
            [scores, jnp.zeros((chunk, pad), F32)], axis=1
        )


def spectra_and_scores(code, wedge_slope, tiles, rot_ref, doms, shells):
    sub_rows = BOX // (doms * shells)
    rows = round_up(2 * sub_rows, 8)
    shifts = tiles.shape[1] - BOX + 1
    angle = 2.0 * math.pi / BOX
    kx = np.arange(BOX)
    phase = angle * ((kx[:, None] * kx[None, :]) % BOX)
    x_table = np.zeros((doms * shells, rows, LANES), np.float32)
    for position in range(doms * shells):
        own = slice(position * sub_rows, (position + 1) * sub_rows)
        x_table[position, :sub_rows, :BOX] = np.cos(phase[own])
        x_table[position, sub_rows : 2 * sub_rows, :BOX] = -np.sin(phase[own])
    y_real = np.zeros((2 * LANES, 2 * BOX), np.float32)
    y_real[:BOX, :BOX] = np.cos(phase)
    y_real[:BOX, BOX:] = -np.sin(phase)
    y_real[LANES : LANES + BOX, :BOX] = np.sin(phase)
    y_real[LANES : LANES + BOX, BOX:] = np.cos(phase)
    gap = 2 * LANES - 2 * BOX
    sides = np.stack([np.pad(y_real, ((0, 0), (0, gap))), np.pad(y_real, ((0, 0), (gap, 0)))])
    high = sides.astype(BF16)
    low = (sides - high.astype(np.float32)).astype(BF16)
    y_table = np.stack([high, low], axis=1)
    particles = code.shape[0]
    depth = rot_ref.shape[1]
    width = round_up(rot_ref.shape[0] + 1, LANES)
    return pl.pallas_call(
        functools.partial(spectra_kernel, sub_rows, shells),
        out_shape=(
            jax.ShapeDtypeStruct((particles, depth), BF16),
            jax.ShapeDtypeStruct((particles, width), F32),
            jax.ShapeDtypeStruct((particles, LANES), BF16),
        ),
        in_specs=[SMEM, SMEM, VMEM, VMEM, VMEM, VMEM],
        out_specs=(VMEM, VMEM, VMEM),
        scratch_shapes=[
            pltpu.VMEM(tiles.shape, BF16),
            pltpu.VMEM((shifts, 2 * rows, LANES), BF16),
            pltpu.VMEM((particles * rows, LANES), F32),
            pltpu.VMEM((particles, LANES), F32),
            pltpu.VMEM((particles, LANES), jnp.int32),
        ],
        compiler_params=pltpu.CompilerParams(vmem_limit_bytes=LIMIT),
        name="spectra_and_scores",
    )(code, wedge_slope, tiles, x_table, y_table, rot_ref)


def softmax_kernel(
    doms, orients, shells, owned, partial_ref, weights_ref, scores, outgoing, s_send, s_recv, w_send, w_recv
):
    count = doms * orients * shells
    dom = lax.axis_index("dom")
    orient = lax.axis_index("orient")
    shell = lax.axis_index("shell")
    me = (dom * orients + orient) * shells + shell
    barrier = pltpu.get_barrier_semaphore()

    def device(index):
        return {
            "dom": index // (orients * shells),
            "orient": (index // shells) % orients,
            "shell": index % shells,
        }

    def each(body):
        @pl.loop(1, count)
        def _(step):
            body(lax.rem(me + step, count))

    def remote(source, target, send_sem, recv_sem, index):
        return pltpu.make_async_remote_copy(
            src_ref=source,
            dst_ref=target,
            send_sem=send_sem,
            recv_sem=recv_sem,
            device_id=device(index),
            device_id_type=MESH,
        )

    each(lambda j: pl.semaphore_signal(barrier, inc=1, device_id=device(j), device_id_type=MESH))
    pl.semaphore_wait(barrier, count - 1)
    each(
        lambda j: remote(
            partial_ref.at[j], scores.at[me], s_send.at[j], s_recv.at[me], j
        ).start()
    )
    scores[me] = partial_ref[me]
    each(
        lambda j: remote(
            partial_ref.at[j], scores.at[j], s_send.at[j], s_recv.at[j], j
        ).wait_recv()
    )
    rows, width = scores.shape[1:]
    lane = lax.broadcasted_iota(jnp.int32, (rows, width), 1)
    real = lane < owned
    halves = []
    for half in range(orients):
        total = jnp.zeros((rows, width), F32)
        for block in range(doms):
            for side in range(shells):
                total = total + scores[(block * orients + half) * shells + side]
        halves.append(jnp.where(real, total * (6.0 / BOX), -3e38))
    top = halves[0]
    for half in halves[1:]:
        top = jnp.maximum(top, half)
    row_top = jnp.max(top, axis=1, keepdims=True)
    shifted = [jnp.where(real, jnp.exp(half - row_top), 0.0) for half in halves]
    row_sum = shifted[0]
    for half in shifted[1:]:
        row_sum = row_sum + half
    row_total = jnp.sum(row_sum, axis=1, keepdims=True)
    logz = row_top + jnp.log(row_total)
    for half in range(orients):
        rounded = (shifted[half] / row_total).astype(BF16).astype(F32)
        outgoing[half] = jnp.where(lane == owned, logz, rounded)
    each(
        lambda j: remote(
            outgoing.at[(j // shells) % orients], weights_ref.at[me], w_send.at[j], w_recv.at[me], j
        ).start()
    )
    weights_ref[me] = outgoing[orient]
    each(
        lambda j: remote(
            outgoing.at[(j // shells) % orients], weights_ref.at[j], w_send.at[j], w_recv.at[j], j
        ).wait_recv()
    )

    def finish(j):
        remote(partial_ref.at[j], scores.at[j], s_send.at[j], s_recv.at[j], j).wait_send()
        remote(
            outgoing.at[(j // shells) % orients], weights_ref.at[j], w_send.at[j], w_recv.at[j], j
        ).wait_send()

    each(finish)


def exchange_softmax(partial_scores, owned, doms, orients, shells):
    count = doms * orients * shells
    particles, width = partial_scores.shape
    blocks = partial_scores.reshape(count, particles // count, width)
    dma = pltpu.SemaphoreType.DMA
    weights = pl.pallas_call(
        functools.partial(softmax_kernel, doms, orients, shells, owned),
        out_shape=jax.ShapeDtypeStruct(blocks.shape, F32),
        in_specs=[VMEM],
        out_specs=VMEM,
        scratch_shapes=[
            pltpu.VMEM(blocks.shape, F32),
            pltpu.VMEM((orients,) + blocks.shape[1:], F32),
            dma((count,)),
            dma((count,)),
            dma((count,)),
            dma((count,)),
        ],
        compiler_params=pltpu.CompilerParams(collective_id=1, has_side_effects=True),
        name="exchange_softmax",
    )(blocks)
    return weights.reshape(particles, width)


def average_kernel(
    sub_rows, shells, owned, slope_ref, weights_ref, weighted_ref, hot_ref, out_ref, logz_ref
):
    dom = lax.axis_index("dom")
    position = dom * shells + lax.axis_index("shell")
    turned = weights_ref[...].T
    part_dev = logz_ref.shape[1]
    particles = turned.shape[1]
    logz_row = jnp.broadcast_to(turned[owned : owned + 1], (8, particles))
    logz_ref[...] = pltpu.roll(logz_row, lax.rem(particles - dom * part_dev, particles), 1)[
        :1, :part_dev
    ]
    kept = turned[:owned].astype(BF16)
    tomo_weight = jnp.dot(kept, hot_ref[...], preferred_element_type=F32)[:, :TOMOS]
    pieces = []
    rest = tomo_weight
    for _ in range(3):
        piece = rest.astype(BF16)
        pieces.append(piece.astype(F32))
        rest = rest - pieces[-1]
    pieces = jnp.concatenate(pieces, axis=1).astype(BF16)
    tomo_row = lax.broadcasted_iota(jnp.int32, (TOMOS, 1), 0)
    slopes = jnp.zeros((TOMOS, 1), F32)
    for tomo in range(TOMOS):
        slopes = jnp.where(tomo_row == tomo, slope_ref[tomo].astype(F32), slopes)
    for row in range(0, sub_rows, 2):
        width = min(2, sub_rows - row) * 2 * BOX
        along_y, along_x = grid_rows(position * sub_rows + row, width)
        wedge = jnp.where(along_y <= slopes * along_x, 1.0, 0.0)
        wedge = jnp.concatenate([wedge, wedge, wedge], axis=0).astype(BF16)
        span = slice(row * 2 * BOX, row * 2 * BOX + width)
        numerator = jnp.dot(kept, weighted_ref[:, span], preferred_element_type=F32)
        denominator = jnp.dot(pieces, wedge, preferred_element_type=F32)
        out_ref[:, span] = numerator / (denominator + 1.0)


def average(wedge_slope, weights, weighted, hot, owned, doms, shells):
    part_dev = weights.shape[0] // doms
    return pl.pallas_call(
        functools.partial(average_kernel, BOX // (doms * shells), shells, owned),
        out_shape=(
            jax.ShapeDtypeStruct((owned, weighted.shape[1]), F32),
            jax.ShapeDtypeStruct((1, part_dev), F32),
        ),
        in_specs=[SMEM, VMEM, VMEM, VMEM],
        out_specs=(VMEM, VMEM),
        compiler_params=pltpu.CompilerParams(vmem_limit_bytes=LIMIT),
        name="average",
    )(wedge_slope, weights, weighted, hot)


def local(tiles, particle_tile, particle_offset, wedge_slope, rot_ref):
    doms = lax.axis_size("dom")
    orients = lax.axis_size("orient")
    shells = lax.axis_size("shell")
    tile_dev, side, _ = tiles.shape
    code = particle_tile * 4096 + particle_offset[:, 0] * 64 + particle_offset[:, 1]
    gathered = gather_tiles(tiles.reshape(tile_dev * side, side), doms, orients, shells)
    weighted, partial_scores, hot = spectra_and_scores(
        code, wedge_slope, gathered.reshape(doms * tile_dev, side, side), rot_ref, doms, shells
    )
    owned = rot_ref.shape[0]
    weights = exchange_softmax(partial_scores, owned, doms, orients, shells)
    new_reference, logz = average(wedge_slope, weights, weighted, hot, owned, doms, shells)
    return new_reference, logz.reshape(-1)


def solution(mesh):
    in_specs = (
        P(("groups", "dom"), None, None),
        P("groups"),
        P("groups", None),
        P("groups"),
        P(("groups", "orient"), ("dom", "shell")),
    )
    out_specs = (P(("groups", "orient"), ("dom", "shell")), P(("groups", "dom")))
    return jax.shard_map(local, mesh=mesh, in_specs=in_specs, out_specs=out_specs, check_vma=False)
```

time: 256 us -> 55.8 us (0.22)
  waiting for transfers between devices: 150 us -> 0 us
  Pallas kernels: 0 us -> 53 us
  matrix products: 35.8 us -> 0 us
  blocking collectives: 23.8 us -> 0 us
  local copies, waits for them, and re-layouts: 21 us -> 0 us
  between operations: 14.3 us -> 0.65 us
  starting transfers between devices: 6.67 us -> 0 us
    all_to_all x1 -> x0, waiting for transfers between devices: 95.7 us -> none  [local(): lax.all_to_all(outgoing, 'dom', split_axis=0, concat_axis=0, tiled=True)]
    reduce_scatter x1 -> x0, waiting for transfers between devices: 53.5 us -> none  [local(): lax.psum_scatter(lax.dot_general(weighted, weights, (((0,), (0,)), ((), (...]
    pallas_call x0 -> x4, Pallas kernels: none -> 53 us  [the longest x1 18.8 us: gather_tiles(): pl.pallas_call(functools.partial(gather_kernel, doms, orients, shells), o...]
    dot_general x20 -> x0, matrix products: 35.8 us -> none  [the longest x1 7.08 us: local(): jnp.einsum('byc,bxc->byx', row_cut, col_select, preferred_element_type=jn...]
    psum x3 -> x0, blocking collectives: 18.8 us -> none  [the longest x1 10.5 us: local(): lax.psum(jnp.dot(tomo_hot.T, weights, preferred_element_type=jnp.float32)...]
    all_to_all x1 -> x0, starting transfers between devices: 6.45 us -> none  [local(): lax.all_to_all(outgoing, 'dom', split_axis=0, concat_axis=0, tiled=True)]
    reshape x3 -> x0, local copies, waits for them, and re-layouts: 5.33 us -> none  [the longest x1 5.09 us: local(): incoming.reshape(dom_count * slot_count, BOX * BOX)]
    convert_element_type x5 -> x0, local copies, waits for them, and re-layouts: 4.95 us -> none  [the longest x4 3.72 us: transform(): return spectrum.reshape(boxes.shape[0], -1).astype(jnp.bfloat16)]
  transfers between devices with their start and end apart: 3 -> 0, of which waited for: 2 -> 0; matrix products, arithmetic and copies ran while one was open for 14% -> 0% of each run, Pallas kernels for 0% -> 0%
where the time goes in v1:
time: 55.8 us; the launch traced here: 55.6 us
  Pallas kernels  53 us (95%)
  other arithmetic  1.98 us (4%)
  between operations  0.65 us (1%)
    pallas_call x1, Pallas kernels, gather_tiles(): pl.pallas_call(functools.partial(gather_kernel, doms, orients, shells), o...  18.8 us
    pallas_call x1, Pallas kernels, spectra_and_scores(): pl.pallas_call(functools.partial(spectra_kernel, sub_rows, shells), out_s...  17 us
    pallas_call x1, Pallas kernels, exchange_softmax(): pl.pallas_call(functools.partial(softmax_kernel, doms, orients, shells, o...  14.4 us
    pallas_call x1, Pallas kernels, average(): pl.pallas_call(functools.partial(average_kernel, BOX // (doms * shells),...  2.89 us
    add x1, other arithmetic, local(): particle_tile * 4096 + particle_offset[:, 0] * 64 + particle_offset[:, 1]  1.22 us

profile of v1, /device:TPU:0, one launch (start us, length us, event | category | flops | bytes accessed | tf_op | source)
XLA Modules:
  0.0 55.6 jit_solution(5712977301044180894)
XLA Ops:
  0.6 0.8 %slice_multiply_fusion = (s32[256,1]{0,1:T(1,128)S(1)}, s32[256,1]{0,1:T(1,128)S(1)}) fusion(s32[256,2]{0,1:T(2,128)} %param.9), kind=kLoop, calls=%fused_computation.1 | loop fusion | flops 256 | bytes 4096 | tf_op jit(solution)/shard_map/mul | solution.py:474
  1.4 1.2 %add_add_fusion.code_ref = s32[256]{0:T(256)} fusion(s32[256]{0:T(256)S(1)} %bitcast.12, s32[256]{0:T(256)S(1)} %bitcast.11, s32[256]{0:T(256)} %param.8), kind=kLoop, calls=%fused_computation | loop fusion | flops 768 | bytes 4096 | tf_op jit(solution)/shard_map/add | solution.py:474
  2.6 18.8 %gather_tiles.1 = bf16[4096,128]{1,0:T(8,128)(2,1)} custom-call(bf16[1024,128]{1,0:T(8,128)(2,1)} %bitcast.9), custom_call_target="tpu_custom_call" | custom-call | tf_op jit(solution)/shard_map/gather_tiles/pallas_call | solution.py:122
  21.4 17.0 %spectra_and_scores.1 = (bf16[256,2304]{1,0:T(8,128)(2,1)}, f32[256,128]{1,0:T(8,128)}, bf16[256,128]{1,0:T(8,128)(2,1)}) custom-call(s32[256]{0:T(256)} %add_add_fusion.code_ref, s32[16]{0:T(128)} %slope_ref.3, bf16[32,128,128]{2,1,0:T(8,128)(2,1)} %bitcast.7, f32[8,24,128]{2,1,0:T(8,128)} %constant.8.clone.x_ref, ...), custom_call_target="tpu_custom_call" | custom-call | tf_op jit(solution)/shard_map/spectra_and_scores/pallas_call | solution.py:284
  38.3 14.4 %exchange_softmax.1 = f32[16,16,128]{2,1,0:T(8,128)} custom-call(f32[16,16,128]{2,1,0:T(8,128)} %bitcast.10), custom_call_target="tpu_custom_call" | custom-call | tf_op jit(solution)/shard_map/exchange_softmax/pallas_call | solution.py:399
  52.7 2.9 %average.1 = (f32[96,2304]{1,0:T(8,128)}, f32[1,64]{1,0:T(1,128)}) custom-call(s32[16]{0:T(128)} %slope_ref.3, f32[256,128]{1,0:T(8,128)} %bitcast.8, bf16[256,2304]{1,0:T(8,128)(2,1)} %get-tuple-element.8.weighted_ref, bf16[256,128]{1,0:T(8,128)(2,1)} %get-tuple-element.9.hot_ref), custom_call_target="tpu_custom_call" | custom-call | tf_op jit(solution)/shard_map/average/pallas_call | solution.py:456

commit v2 on v1

v2 whole, which is shorter than its diff:
```python
import functools
import math

import jax
import jax.numpy as jnp
import numpy as np
from jax import lax
from jax.experimental import pallas as pl
from jax.experimental.pallas import tpu as pltpu
from jax.sharding import PartitionSpec as P

BOX = 96
TOMOS = 16
LANES = 128
MESH = pl.DeviceIdType.MESH
VMEM = pl.BlockSpec(memory_space=pltpu.VMEM)
SMEM = pl.BlockSpec(memory_space=pltpu.SMEM)
F32 = jnp.float32
BF16 = jnp.bfloat16
LIMIT = 56 * 1024 * 1024


def round_up(value, step):
    return -(-value // step) * step


def split(values):
    pieces = []
    for _ in range(3):
        pieces.append(values.astype(BF16))
        values = values - pieces[-1].astype(F32)
    return pieces


def grid_rows(kx_first, width):
    lane = lax.broadcasted_iota(jnp.int32, (1, width), 1)
    kx_step = jnp.zeros_like(lane)
    ky = lane
    for edge in range(BOX, width, BOX):
        over = (lane >= edge).astype(jnp.int32)
        ky = ky - BOX * over
        if edge % (2 * BOX) == 0:
            kx_step = kx_step + over
    kx = kx_first + kx_step
    along_y = jnp.minimum(ky, BOX - ky) * 100
    along_x = jnp.minimum(kx, BOX - kx)
    return along_y.astype(F32), along_x.astype(F32)


def gather_tiles(peers, mine_ref, all_ref, sems):
    doms, orients, shells = peers
    z_send, z_recv, x_send, x_recv, c_send, c_recv = sems
    dom = lax.axis_index("dom")
    orient = lax.axis_index("orient")
    shell = lax.axis_index("shell")
    rows = mine_ref.shape[0]
    piece = rows // (orients * shells)
    z_peers = [lax.rem(dom + r, doms) for r in range(1, doms)]
    x_peers = [lax.rem(orient + r, orients) for r in range(1, orients)]
    c_peers = [lax.rem(shell + r, shells) for r in range(1, shells)]

    def part(block, x, c):
        start = pl.multiple_of(block * rows + (x * shells + c) * piece, 16)
        return all_ref.at[pl.ds(start, piece)]

    first = pl.multiple_of((orient * shells + shell) * piece, 16)
    started = []

    def send(source, target, send_sem, recv_sem, device):
        copy = pltpu.make_async_remote_copy(
            src_ref=source,
            dst_ref=target,
            send_sem=send_sem,
            recv_sem=recv_sem,
            device_id=device,
            device_id_type=MESH,
        )
        copy.start()
        started.append(copy)

    def arrived(target, send_sem, recv_sem, device):
        pltpu.make_async_remote_copy(
            src_ref=target,
            dst_ref=target,
            send_sem=send_sem,
            recv_sem=recv_sem,
            device_id=device,
            device_id_type=MESH,
        ).wait_recv()

    for r, z in enumerate(z_peers):
        send(
            mine_ref.at[pl.ds(first, piece)],
            part(dom, orient, shell),
            z_send.at[r],
            z_recv.at[dom],
            {"dom": z},
        )
    yield None
    for r, z in enumerate(z_peers):
        held = part(z, orient, shell)
        arrived(held, z_send.at[r], z_recv.at[z], {"dom": z})
        for i, x in enumerate(x_peers):
            send(held, held, x_send.at[r, i], x_recv.at[z, orient], {"orient": x})
        for i, c in enumerate(c_peers):
            send(held, held, c_send.at[r, 0, i], c_recv.at[z, orient, shell], {"shell": c})
    for r, z in enumerate(z_peers):
        for k, x in enumerate(x_peers):
            held = part(z, x, shell)
            arrived(held, x_send.at[r, k], x_recv.at[z, x], {"orient": x})
            for i, c in enumerate(c_peers):
                send(held, held, c_send.at[r, 1 + k, i], c_recv.at[z, x, shell], {"shell": c})
    for r, z in enumerate(z_peers):
        for k in range(orients):
            x = lax.rem(orient + k, orients)
            for i, c in enumerate(c_peers):
                arrived(part(z, x, c), c_send.at[r, k, i], c_recv.at[z, x, c], {"shell": c})
        yield z
    for copy in started:
        copy.wait_send()


def assign_kernel(
    peers,
    sub_rows,
    owned,
    code_ref,
    slope_ref,
    mine_ref,
    x_ref,
    y_ref,
    rot_ref,
    weighted_ref,
    weights_ref,
    hot_ref,
    tiles_ref,
    tile_t,
    x_tab,
    held,
    slopes,
    tomos,
    partial_ref,
    scores,
    outgoing,
    z_send,
    z_recv,
    x_send,
    x_recv,
    c_send,
    c_recv,
    s_send,
    s_recv,
    w_send,
    w_recv,
):
    doms, orients, shells = peers
    count = doms * orients * shells
    dom = lax.axis_index("dom")
    orient = lax.axis_index("orient")
    shell = lax.axis_index("shell")
    me = (dom * orients + orient) * shells + shell
    position = dom * shells + shell
    barrier = pltpu.get_barrier_semaphore()

    def device(index):
        return {
            "dom": index // (orients * shells),
            "orient": (index // shells) % orients,
            "shell": index % shells,
        }

    def each(body):
        @pl.loop(1, count)
        def _(step):
            body(lax.rem(me + step, count))

    def remote(source, target, send_sem, recv_sem, index):
        return pltpu.make_async_remote_copy(
            src_ref=source,
            dst_ref=target,
            send_sem=send_sem,
            recv_sem=recv_sem,
            device_id=device(index),
            device_id_type=MESH,
        )

    each(lambda j: pl.semaphore_signal(barrier, inc=1, device_id=device(j), device_id_type=MESH))
    pl.semaphore_wait(barrier, count - 1)

    side = tile_t.shape[1]
    tile_dev = mine_ref.shape[0] // side
    gather = gather_tiles(
        peers, mine_ref, tiles_ref, (z_send, z_recv, x_send, x_recv, c_send, c_recv)
    )
    next(gather)

    rows = x_ref.shape[1]
    particles = slopes.shape[0]
    base = x_ref[position]
    for shift in range(x_tab.shape[0]):
        moved = base if shift == 0 else pltpu.roll(base, shift, 1)
        pieces = [piece.astype(F32) for piece in split(moved)]
        filler = x_tab.shape[1] - 3 * rows
        if filler:
            pieces.append(jnp.zeros((filler, LANES), F32))
        x_tab[shift] = jnp.concatenate(pieces, axis=0).astype(BF16)

    @pl.loop(0, tile_dev)
    def _(tile):
        own = mine_ref[pl.ds(pl.multiple_of(tile * side, side), side), :]
        tile_t[dom * tile_dev + tile] = own.astype(F32).T.astype(BF16)

    for block in gather:

        @pl.loop(0, tile_dev)
        def _(tile):
            index = block * tile_dev + tile
            own = tiles_ref[pl.ds(pl.multiple_of(index * side, side), side), :]
            tile_t[index] = own.astype(F32).T.astype(BF16)

    unroll = 8

    @pl.loop(0, particles // unroll)
    def _(step):
        for part in range(unroll):
            particle = step * unroll + part
            code = code_ref[particle]
            tile = code >> 12
            start_y = (code >> 6) & 63
            start_x = code & 63
            both = jnp.dot(x_tab[start_x], tile_t[tile], preferred_element_type=F32)
            along = both[:rows] + (both[rows : 2 * rows] + both[2 * rows : 3 * rows])
            along = pltpu.roll(along, (LANES - start_y) & (LANES - 1), 1)
            held[pl.ds(pl.multiple_of(particle * rows, 8), rows), :] = along
            tomo = tile & (TOMOS - 1)
            slope = slope_ref[tomo].astype(F32)
            slopes[pl.ds(particle, 1), :] = jnp.full((1, LANES), slope, F32)
            tomos[pl.ds(particle, 1), :] = jnp.full((1, LANES), tomo, jnp.int32)

    lane = lax.broadcasted_iota(jnp.int32, tomos.shape, 1)
    hot_ref[...] = jnp.where(tomos[...] == lane, 1.0, 0.0).astype(BF16)
    kx_first = position * sub_rows
    share = scores.shape[1]
    chunk = 256

    @pl.loop(0, particles // chunk)
    def _(block):
        first = pl.multiple_of(block * chunk, chunk)
        own_slope = slopes[pl.ds(first, chunk), :][:, :1]

        def lines(row, which):
            real = held[pl.ds(first * rows + row, chunk, stride=rows), :]
            imag = held[pl.ds(first * rows + sub_rows + row, chunk, stride=rows), :]
            high, middle, low = split(jnp.concatenate([real, imag], axis=1))

            def times(piece, table):
                return jnp.dot(piece, y_ref[which, table], preferred_element_type=F32)

            small = times(high, 2) + times(low, 0) + times(middle, 1)
            return times(high, 0) + (times(high, 1) + times(middle, 0) + small)

        for row in range(0, sub_rows, 2):
            even = lines(row, 0)
            if row + 1 < sub_rows:
                odd = lines(row + 1, 1)
                values = jnp.concatenate(
                    [even[:, :LANES], even[:, LANES:] + odd[:, :LANES], odd[:, LANES:]], axis=1
                )
            else:
                values = even[:, : 2 * BOX]
            width = values.shape[1]
            along_y, along_x = grid_rows(kx_first + row, width)
            inside = along_y <= own_slope * along_x
            values = jnp.where(inside, values * (1.0 / BOX), 0.0)
            weighted_ref[pl.ds(first, chunk), row * 2 * BOX : row * 2 * BOX + width] = values.astype(
                BF16
            )
        result = lax.dot_general(
            weighted_ref[pl.ds(first, chunk), :],
            rot_ref[...],
            (((1,), (1,)), ((), ())),
            preferred_element_type=F32,
        )
        pad = partial_ref.shape[2] - owned
        result = jnp.concatenate([result, jnp.zeros((chunk, pad), F32)], axis=1)
        for line in range(chunk // share):
            partial_ref[block * (chunk // share) + line] = result[line * share : (line + 1) * share]

    each(
        lambda j: remote(
            partial_ref.at[j], scores.at[me], s_send.at[j], s_recv.at[me], j
        ).start()
    )
    scores[me] = partial_ref[me]
    each(
        lambda j: remote(
            partial_ref.at[j], scores.at[j], s_send.at[j], s_recv.at[j], j
        ).wait_recv()
    )
    width = scores.shape[2]
    lane = lax.broadcasted_iota(jnp.int32, (share, width), 1)
    real = lane < owned
    halves = []
    for half in range(orients):
        total = jnp.zeros((share, width), F32)
        for block in range(doms):
            for c in range(shells):
                total = total + scores[(block * orients + half) * shells + c]
        halves.append(jnp.where(real, total * (6.0 / BOX), -3e38))
    top = halves[0]
    for half in halves[1:]:
        top = jnp.maximum(top, half)
    row_top = jnp.max(top, axis=1, keepdims=True)
    shifted = [jnp.where(real, jnp.exp(half - row_top), 0.0) for half in halves]
    row_sum = shifted[0]
    for half in shifted[1:]:
        row_sum = row_sum + half
    row_total = jnp.sum(row_sum, axis=1, keepdims=True)
    logz = row_top + jnp.log(row_total)
    for half in range(orients):
        rounded = (shifted[half] / row_total).astype(BF16).astype(F32)
        outgoing[half] = jnp.where(lane == owned, logz, rounded)
    each(
        lambda j: remote(
            outgoing.at[(j // shells) % orients], weights_ref.at[me], w_send.at[j], w_recv.at[me], j
        ).start()
    )
    weights_ref[me] = outgoing[orient]
    each(
        lambda j: remote(
            outgoing.at[(j // shells) % orients], weights_ref.at[j], w_send.at[j], w_recv.at[j], j
        ).wait_recv()
    )

    def finish(j):
        remote(partial_ref.at[j], scores.at[j], s_send.at[j], s_recv.at[j], j).wait_send()
        remote(
            outgoing.at[(j // shells) % orients], weights_ref.at[j], w_send.at[j], w_recv.at[j], j
        ).wait_send()

    each(finish)


def assign(code, wedge_slope, tiles, rot_ref, peers):
    doms, orients, shells = peers
    count = doms * orients * shells
    tile_dev, side, _ = tiles.shape
    sub_rows = BOX // (doms * shells)
    rows = round_up(2 * sub_rows, 8)
    shifts = side - BOX + 1
    angle = 2.0 * math.pi / BOX
    kx = np.arange(BOX)
    phase = angle * ((kx[:, None] * kx[None, :]) % BOX)
    x_table = np.zeros((doms * shells, rows, LANES), np.float32)
    for position in range(doms * shells):
        own = slice(position * sub_rows, (position + 1) * sub_rows)
        x_table[position, :sub_rows, :BOX] = np.cos(phase[own])
        x_table[position, sub_rows : 2 * sub_rows, :BOX] = -np.sin(phase[own])
    y_real = np.zeros((2 * LANES, 2 * BOX), np.float32)
    y_real[:BOX, :BOX] = np.cos(phase)
    y_real[:BOX, BOX:] = -np.sin(phase)
    y_real[LANES : LANES + BOX, :BOX] = np.sin(phase)
    y_real[LANES : LANES + BOX, BOX:] = np.cos(phase)
    gap = 2 * LANES - 2 * BOX
    rest = np.stack([np.pad(y_real, ((0, 0), (0, gap))), np.pad(y_real, ((0, 0), (gap, 0)))])
    y_table = []
    for _ in range(3):
        y_table.append(rest.astype(BF16))
        rest = rest - y_table[-1].astype(np.float32)
    y_table = np.stack(y_table, axis=1)
    particles = code.shape[0]
    owned, depth = rot_ref.shape
    width = round_up(owned + 1, LANES)
    blocks = (count, particles // count, width)
    dma = pltpu.SemaphoreType.DMA
    weighted, weights, hot = pl.pallas_call(
        functools.partial(assign_kernel, peers, sub_rows, owned),
        out_shape=(
            jax.ShapeDtypeStruct((particles, depth), BF16),
            jax.ShapeDtypeStruct(blocks, F32),
            jax.ShapeDtypeStruct((particles, LANES), BF16),
        ),
        in_specs=[SMEM, SMEM, VMEM, VMEM, VMEM, VMEM],
        out_specs=(VMEM, VMEM, VMEM),
        scratch_shapes=[
            pltpu.VMEM((doms * tile_dev * side, side), BF16),
            pltpu.VMEM((doms * tile_dev, side, side), BF16),
            pltpu.VMEM((shifts, round_up(3 * rows, 16), LANES), BF16),
            pltpu.VMEM((particles * rows, LANES), F32),
            pltpu.VMEM((particles, LANES), F32),
            pltpu.VMEM((particles, LANES), jnp.int32),
            pltpu.VMEM(blocks, F32),
            pltpu.VMEM(blocks, F32),
            pltpu.VMEM((orients,) + blocks[1:], F32),
            dma((doms,)),
            dma((doms,)),
            dma((doms, orients)),
            dma((doms, orients)),
            dma((doms, orients, shells)),
            dma((doms, orients, shells)),
            dma((count,)),
            dma((count,)),
            dma((count,)),
            dma((count,)),
        ],
        compiler_params=pltpu.CompilerParams(
            collective_id=0, has_side_effects=True, vmem_limit_bytes=LIMIT
        ),
        name="assign",
    )(code, wedge_slope, tiles.reshape(tile_dev * side, side), x_table, y_table, rot_ref)
    return weighted, weights.reshape(particles, width), hot


def average_kernel(
    sub_rows, shells, owned, slope_ref, weights_ref, weighted_ref, hot_ref, out_ref, logz_ref
):
    dom = lax.axis_index("dom")
    position = dom * shells + lax.axis_index("shell")
    turned = weights_ref[...].T
    part_dev = logz_ref.shape[1]
    particles = turned.shape[1]
    logz_row = jnp.broadcast_to(turned[owned : owned + 1], (8, particles))
    logz_ref[...] = pltpu.roll(logz_row, lax.rem(particles - dom * part_dev, particles), 1)[
        :1, :part_dev
    ]
    kept = turned[:owned].astype(BF16)
    tomo_weight = jnp.dot(kept, hot_ref[...], preferred_element_type=F32)[:, :TOMOS]
    pieces = []
    rest = tomo_weight
    for _ in range(3):
        piece = rest.astype(BF16)
        pieces.append(piece.astype(F32))
        rest = rest - pieces[-1]
    pieces = jnp.concatenate(pieces, axis=1).astype(BF16)
    tomo_row = lax.broadcasted_iota(jnp.int32, (TOMOS, 1), 0)
    slopes = jnp.zeros((TOMOS, 1), F32)
    for tomo in range(TOMOS):
        slopes = jnp.where(tomo_row == tomo, slope_ref[tomo].astype(F32), slopes)
    for row in range(0, sub_rows, 2):
        width = min(2, sub_rows - row) * 2 * BOX
        along_y, along_x = grid_rows(position * sub_rows + row, width)
        wedge = jnp.where(along_y <= slopes * along_x, 1.0, 0.0)
        wedge = jnp.concatenate([wedge, wedge, wedge], axis=0).astype(BF16)
        span = slice(row * 2 * BOX, row * 2 * BOX + width)
        numerator = jnp.dot(kept, weighted_ref[:, span], preferred_element_type=F32)
        denominator = jnp.dot(pieces, wedge, preferred_element_type=F32)
        out_ref[:, span] = numerator / (denominator + 1.0)


def average(wedge_slope, weights, weighted, hot, owned, doms, shells):
    part_dev = weights.shape[0] // doms
    return pl.pallas_call(
        functools.partial(average_kernel, BOX // (doms * shells), shells, owned),
        out_shape=(
            jax.ShapeDtypeStruct((owned, weighted.shape[1]), F32),
            jax.ShapeDtypeStruct((1, part_dev), F32),
        ),
        in_specs=[SMEM, VMEM, VMEM, VMEM],
        out_specs=(VMEM, VMEM),
        compiler_params=pltpu.CompilerParams(vmem_limit_bytes=LIMIT),
        name="average",
    )(wedge_slope, weights, weighted, hot)


def local(tiles, particle_tile, particle_offset, wedge_slope, rot_ref):
    doms = lax.axis_size("dom")
    orients = lax.axis_size("orient")
    shells = lax.axis_size("shell")
    packing = jnp.array([64, 1], jnp.int32)
    code = particle_tile * 4096 + jnp.sum(particle_offset * packing[None, :], axis=1)
    weighted, weights, hot = assign(code, wedge_slope, tiles, rot_ref, (doms, orients, shells))
    owned = rot_ref.shape[0]
    new_reference, logz = average(wedge_slope, weights, weighted, hot, owned, doms, shells)
    return new_reference, logz.reshape(-1)


def solution(mesh):
    in_specs = (
        P(("groups", "dom"), None, None),
        P("groups"),
        P("groups", None),
        P("groups"),
        P(("groups", "orient"), ("dom", "shell")),
    )
    out_specs = (P(("groups", "orient"), ("dom", "shell")), P(("groups", "dom")))
    return jax.shard_map(local, mesh=mesh, in_specs=in_specs, out_specs=out_specs, check_vma=False)
```

time: 55.8 us -> 52.6 us (0.943)
  Pallas kernels: 53 us -> 49.8 us
    pallas_call x3 -> x1, Pallas kernels: 50.1 us -> 46.9 us  [assign(): pl.pallas_call(functools.partial(assign_kernel, peers, sub_rows, owned),...]
    reduce_sum x0 -> x1, other arithmetic: none -> 0.77 us  [local(): jnp.sum(particle_offset * packing[None, :], axis=1)]
    mul x1 -> x0, other arithmetic: 0.76 us -> none  [local(): particle_offset[:, 0] * 64]
where the time goes in v2:
time: 52.6 us; the launch traced here: 52.4 us
  Pallas kernels  49.8 us (95%)
  other arithmetic  2.01 us (4%)
  between operations  0.64 us (1%)
    pallas_call x1, Pallas kernels, assign(): pl.pallas_call(functools.partial(assign_kernel, peers, sub_rows, owned),...  46.9 us
    pallas_call x1, Pallas kernels, average(): pl.pallas_call(functools.partial(average_kernel, BOX // (doms * shells),...  2.89 us
    add x1, other arithmetic, local(): particle_tile * 4096 + jnp.sum(particle_offset * packing[None, :], axis=1)  1.24 us

profile of v2, /device:TPU:0, one launch (start us, length us, event | category | flops | bytes accessed | tf_op | source)
XLA Modules:
  0.0 52.4 jit_solution(13819311996986607329)
XLA Ops:
  0.6 0.8 %multiply_reduce_fusion = s32[256]{0:T(256)S(1)} fusion(s32[256,2]{0,1:T(2,128)} %param.10, s32[2]{0:T(128)} %constant.10.clone), kind=kLoop, calls=%fused_computation | loop fusion | flops 768 | bytes 3080 | tf_op jit(solution)/shard_map/reduce_sum | solution.py:470
  1.4 1.2 %multiply_add_fusion.code_ref = s32[256]{0:T(256)} fusion(s32[256]{0:T(256)S(1)} %multiply_reduce_fusion, s32[256]{0:T(256)} %param.9), kind=kLoop, calls=%fused_computation.1 | loop fusion | flops 512 | bytes 3072 | tf_op jit(solution)/shard_map/add | solution.py:470
  2.6 46.9 %assign.1 = (bf16[256,2304]{1,0:T(8,128)(2,1)}, f32[16,16,128]{2,1,0:T(8,128)}, bf16[256,128]{1,0:T(8,128)(2,1)}) custom-call(s32[256]{0:T(256)} %multiply_add_fusion.code_ref, s32[16]{0:T(128)} %slope_ref.3, bf16[1024,128]{1,0:T(8,128)(2,1)} %bitcast.3, f32[8,24,128]{2,1,0:T(8,128)} %constant.11.clone.x_ref, bf16[2,3,256,256]{3,2,1,0:T(8,128)(2,1)} %constant.12.clone.y_ref, ...), custom_call_target="tpu_custom_call" | custom-call | tf_op jit(solution)/shard_map/assign/pallas_call | solution.py:376
  49.5 2.9 %average.1 = (f32[96,2304]{1,0:T(8,128)}, f32[1,64]{1,0:T(1,128)}) custom-call(s32[16]{0:T(128)} %slope_ref.3, f32[256,128]{1,0:T(8,128)} %bitcast.4, bf16[256,2304]{1,0:T(8,128)(2,1)} %get-tuple-element.8.weighted_ref, bf16[256,128]{1,0:T(8,128)(2,1)} %get-tuple-element.9.hot_ref), custom_call_target="tpu_custom_call" | custom-call | tf_op jit(solution)/shard_map/average/pallas_call | solution.py:452

commit v3 on v2

--- a/solution.py
+++ b/solution.py
@@ -14,6 +14,7 @@
 LANES = 128
 MESH = pl.DeviceIdType.MESH
 VMEM = pl.BlockSpec(memory_space=pltpu.VMEM)
+ANY = pl.BlockSpec(memory_space=pl.ANY)
 SMEM = pl.BlockSpec(memory_space=pltpu.SMEM)
 F32 = jnp.float32
 BF16 = jnp.bfloat16
@@ -124,15 +125,20 @@
     peers,
     sub_rows,
     owned,
-    code_ref,
+    tile_ref,
+    offset_ref,
     slope_ref,
     mine_ref,
     x_ref,
+    y_hbm,
+    rot_hbm,
+    weighted_hbm,
+    weights_ref,
+    hot_ref,
     y_ref,
     rot_ref,
     weighted_ref,
-    weights_ref,
-    hot_ref,
+    l_sem,
     tiles_ref,
     tile_t,
     x_tab,
@@ -162,29 +168,61 @@
     position = dom * shells + shell
     barrier = pltpu.get_barrier_semaphore()
 
-    def device(index):
-        return {
-            "dom": index // (orients * shells),
-            "orient": (index // shells) % orients,
-            "shell": index % shells,
-        }
+    def near(z, skip):
+        found = []
+        for x in range(orients):
+            for c in range(shells):
+                if skip and x == 0 and c == 0:
+                    continue
+                found.append((z, lax.rem(orient + x, orients), lax.rem(shell + c, shells)))
+        return found
 
     def each(body):
-        @pl.loop(1, count)
-        def _(step):
-            body(lax.rem(me + step, count))
-
-    def remote(source, target, send_sem, recv_sem, index):
+        if doms > 4:
+
+            @pl.loop(1, doms)
+            def _(step):
+                for peer in near(lax.rem(dom + step, doms), False):
+                    body(peer)
+
+        else:
+            for step in range(1, doms):
+                for peer in near(lax.rem(dom + step, doms), False):
+                    body(peer)
+        for peer in near(dom, True):
+            body(peer)
+
+    def number(peer):
+        return (peer[0] * orients + peer[1]) * shells + peer[2]
+
+    def device(peer):
+        return {"dom": peer[0], "orient": peer[1], "shell": peer[2]}
+
+    def remote(source, target, send_sem, recv_sem, peer):
         return pltpu.make_async_remote_copy(
             src_ref=source,
             dst_ref=target,
             send_sem=send_sem,
             recv_sem=recv_sem,
-            device_id=device(index),
+            device_id=device(peer),
             device_id_type=MESH,
         )
 
+    def part_copy(peer, slot):
+        j = number(peer)
+        return remote(partial_ref.at[j], scores.at[slot], s_send.at[j], s_recv.at[slot], peer)
+
+    def weight_copy(peer, slot):
+        j = number(peer)
+        return remote(
+            outgoing.at[peer[1]], weights_ref.at[slot], w_send.at[j], w_recv.at[slot], peer
+        )
+
     each(lambda j: pl.semaphore_signal(barrier, inc=1, device_id=device(j), device_id_type=MESH))
+    y_copy = pltpu.make_async_copy(y_hbm, y_ref, l_sem.at[0])
+    rot_copy = pltpu.make_async_copy(rot_hbm, rot_ref, l_sem.at[1])
+    y_copy.start()
+    rot_copy.start()
     pl.semaphore_wait(barrier, count - 1)
 
     side = tile_t.shape[1]
@@ -218,16 +256,15 @@
             own = tiles_ref[pl.ds(pl.multiple_of(index * side, side), side), :]
             tile_t[index] = own.astype(F32).T.astype(BF16)
 
-    unroll = 8
+    unroll = 16
 
     @pl.loop(0, particles // unroll)
     def _(step):
         for part in range(unroll):
             particle = step * unroll + part
-            code = code_ref[particle]
-            tile = code >> 12
-            start_y = (code >> 6) & 63
-            start_x = code & 63
+            tile = tile_ref[particle]
+            start_y = offset_ref[0, particle]
+            start_x = offset_ref[1, particle]
             both = jnp.dot(x_tab[start_x], tile_t[tile], preferred_element_type=F32)
             along = both[:rows] + (both[rows : 2 * rows] + both[2 * rows : 3 * rows])
             along = pltpu.roll(along, (LANES - start_y) & (LANES - 1), 1)
@@ -237,6 +274,8 @@
             slopes[pl.ds(particle, 1), :] = jnp.full((1, LANES), slope, F32)
             tomos[pl.ds(particle, 1), :] = jnp.full((1, LANES), tomo, jnp.int32)
 
+    y_copy.wait()
+    rot_copy.wait()
     lane = lax.broadcasted_iota(jnp.int32, tomos.shape, 1)
     hot_ref[...] = jnp.where(tomos[...] == lane, 1.0, 0.0).astype(BF16)
     kx_first = position * sub_rows
@@ -286,17 +325,11 @@
         for line in range(chunk // share):
             partial_ref[block * (chunk // share) + line] = result[line * share : (line + 1) * share]
 
-    each(
-        lambda j: remote(
-            partial_ref.at[j], scores.at[me], s_send.at[j], s_recv.at[me], j
-        ).start()
-    )
+    out_copy = pltpu.make_async_copy(weighted_ref, weighted_hbm, l_sem.at[2])
+    each(lambda peer: part_copy(peer, me).start())
+    out_copy.start()
     scores[me] = partial_ref[me]
-    each(
-        lambda j: remote(
-            partial_ref.at[j], scores.at[j], s_send.at[j], s_recv.at[j], j
-        ).wait_recv()
-    )
+    each(lambda peer: part_copy(peer, number(peer)).wait_recv())
     width = scores.shape[2]
     lane = lax.broadcasted_iota(jnp.int32, (share, width), 1)
     real = lane < owned
@@ -320,28 +353,19 @@
     for half in range(orients):
         rounded = (shifted[half] / row_total).astype(BF16).astype(F32)
         outgoing[half] = jnp.where(lane == owned, logz, rounded)
-    each(
-        lambda j: remote(
-            outgoing.at[(j // shells) % orients], weights_ref.at[me], w_send.at[j], w_recv.at[me], j
-        ).start()
-    )
+    each(lambda peer: weight_copy(peer, me).start())
     weights_ref[me] = outgoing[orient]
-    each(
-        lambda j: remote(
-            outgoing.at[(j // shells) % orients], weights_ref.at[j], w_send.at[j], w_recv.at[j], j
-        ).wait_recv()
-    )
-
-    def finish(j):
-        remote(partial_ref.at[j], scores.at[j], s_send.at[j], s_recv.at[j], j).wait_send()
-        remote(
-            outgoing.at[(j // shells) % orients], weights_ref.at[j], w_send.at[j], w_recv.at[j], j
-        ).wait_send()
-
+    out_copy.wait()
+
+    def finish(peer):
+        part_copy(peer, me).wait_send()
+        weight_copy(peer, me).wait_send()
+
+    each(lambda peer: weight_copy(peer, number(peer)).wait_recv())
     each(finish)
 
 
-def assign(code, wedge_slope, tiles, rot_ref, peers):
+def assign(particle_tile, particle_offset, wedge_slope, tiles, rot_ref, peers):
     doms, orients, shells = peers
     count = doms * orients * shells
     tile_dev, side, _ = tiles.shape
@@ -368,7 +392,7 @@
         y_table.append(rest.astype(BF16))
         rest = rest - y_table[-1].astype(np.float32)
     y_table = np.stack(y_table, axis=1)
-    particles = code.shape[0]
+    particles = particle_tile.shape[0]
     owned, depth = rot_ref.shape
     width = round_up(owned + 1, LANES)
     blocks = (count, particles // count, width)
@@ -380,9 +404,13 @@
             jax.ShapeDtypeStruct(blocks, F32),
             jax.ShapeDtypeStruct((particles, LANES), BF16),
         ),
-        in_specs=[SMEM, SMEM, VMEM, VMEM, VMEM, VMEM],
-        out_specs=(VMEM, VMEM, VMEM),
+        in_specs=[SMEM, SMEM, SMEM, VMEM, VMEM, ANY, ANY],
+        out_specs=(ANY, VMEM, VMEM),
         scratch_shapes=[
+            pltpu.VMEM(y_table.shape, BF16),
+            pltpu.VMEM(rot_ref.shape, BF16),
+            pltpu.VMEM((particles, depth), BF16),
+            dma((3,)),
             pltpu.VMEM((doms * tile_dev * side, side), BF16),
             pltpu.VMEM((doms * tile_dev, side, side), BF16),
             pltpu.VMEM((shifts, round_up(3 * rows, 16), LANES), BF16),
@@ -407,7 +435,7 @@
             collective_id=0, has_side_effects=True, vmem_limit_bytes=LIMIT
         ),
         name="assign",
-    )(code, wedge_slope, tiles.reshape(tile_dev * side, side), x_table, y_table, rot_ref)
+    )(particle_tile, particle_offset.T, wedge_slope, tiles.reshape(tile_dev * side, side), x_table, y_table, rot_ref)
     return weighted, weights.reshape(particles, width), hot
 
 
@@ -466,9 +494,9 @@
     doms = lax.axis_size("dom")
     orients = lax.axis_size("orient")
     shells = lax.axis_size("shell")
-    packing = jnp.array([64, 1], jnp.int32)
-    code = particle_tile * 4096 + jnp.sum(particle_offset * packing[None, :], axis=1)
-    weighted, weights, hot = assign(code, wedge_slope, tiles, rot_ref, (doms, orients, shells))
+    weighted, weights, hot = assign(
+        particle_tile, particle_offset, wedge_slope, tiles, rot_ref, (doms, orients, shells)
+    )
     owned = rot_ref.shape[0]
     new_reference, logz = average(wedge_slope, weights, weighted, hot, owned, doms, shells)
     return new_reference, logz.reshape(-1)

time: 52.6 us -> 46.2 us (0.88)
  Pallas kernels: 49.8 us -> 45.4 us
  other arithmetic: 2.01 us -> 0 us
    pallas_call x1, Pallas kernels: 46.9 us -> 42.5 us  [assign(): pl.pallas_call(functools.partial(assign_kernel, peers, sub_rows, owned),...]
    add x1 -> x0, other arithmetic: 1.24 us -> none  [local(): particle_tile * 4096 + jnp.sum(particle_offset * packing[None, :], axis=1)]
    reduce_sum x1 -> x0, other arithmetic: 0.77 us -> none  [local(): jnp.sum(particle_offset * packing[None, :], axis=1)]
where the time goes in v3:
time: 46.2 us; the launch traced here: 46 us
  Pallas kernels  45.4 us (98%)
  between operations  0.64 us (1%)
    pallas_call x1, Pallas kernels, assign(): pl.pallas_call(functools.partial(assign_kernel, peers, sub_rows, owned),...  42.5 us
    pallas_call x1, Pallas kernels, average(): pl.pallas_call(functools.partial(average_kernel, BOX // (doms * shells),...  2.89 us

profile of v3, /device:TPU:0, one launch (start us, length us, event | category | flops | bytes accessed | tf_op | source)
XLA Modules:
  0.0 46.0 jit_solution(6962378928555319566)
XLA Ops:
  0.6 42.5 %assign.1 = (bf16[256,2304]{1,0:T(8,128)(2,1)}, f32[16,16,128]{2,1,0:T(8,128)}, bf16[256,128]{1,0:T(8,128)(2,1)}) custom-call(s32[256]{0:T(256)} %tile_ref.1, s32[2,256]{1,0:T(2,128)} %bitcast.6, s32[16]{0:T(128)} %slope_ref.3, bf16[1024,128]{1,0:T(8,128)(2,1)} %bitcast.4, f32[8,24,128]{2,1,0:T(8,128)} %constant.4.clone.x_ref, ...), custom_call_target="tpu_custom_call" | custom-call | tf_op jit(solution)/shard_map/assign/pallas_call | solution.py:400
  43.1 2.9 %average.1 = (f32[96,2304]{1,0:T(8,128)}, f32[1,64]{1,0:T(1,128)}) custom-call(s32[16]{0:T(128)} %slope_ref.3, f32[256,128]{1,0:T(8,128)} %bitcast.5, bf16[256,2304]{1,0:T(8,128)(2,1)} %get-tuple-element.8.weighted_ref, bf16[256,128]{1,0:T(8,128)(2,1)} %get-tuple-element.9.hot_ref), custom_call_target="tpu_custom_call" | custom-call | tf_op jit(solution)/shard_map/average/pallas_call | solution.py:480

commit v4 on v3

--- a/solution.py
+++ b/solution.py
@@ -56,7 +56,8 @@
     shell = lax.axis_index("shell")
     rows = mine_ref.shape[0]
     piece = rows // (orients * shells)
-    z_peers = [lax.rem(dom + r, doms) for r in range(1, doms)]
+    far_first = sorted(range(1, doms), key=lambda r: -min(r, doms - r))
+    z_peers = [lax.rem(dom + r, doms) for r in far_first]
     x_peers = [lax.rem(orient + r, orients) for r in range(1, orients)]
     c_peers = [lax.rem(shell + r, shells) for r in range(1, shells)]
 
@@ -134,6 +135,7 @@
     rot_hbm,
     weighted_hbm,
     weights_ref,
+    logz_ref,
     hot_ref,
     y_ref,
     rot_ref,
@@ -158,6 +160,8 @@
     s_recv,
     w_send,
     w_recv,
+    g_send,
+    g_recv,
 ):
     doms, orients, shells = peers
     count = doms * orients * shells
@@ -217,6 +221,11 @@
         return remote(
             outgoing.at[peer[1]], weights_ref.at[slot], w_send.at[j], w_recv.at[slot], peer
         )
+
+    def logz_copy(peer, slot):
+        q = peer[1] * shells + peer[2]
+        block = logz_ref.at[slot]
+        return remote(block, block, g_send.at[q], g_recv.at[slot], peer)
 
     each(lambda j: pl.semaphore_signal(barrier, inc=1, device_id=device(j), device_id_type=MESH))
     y_copy = pltpu.make_async_copy(y_hbm, y_ref, l_sem.at[0])
@@ -256,7 +265,7 @@
             own = tiles_ref[pl.ds(pl.multiple_of(index * side, side), side), :]
             tile_t[index] = own.astype(F32).T.astype(BF16)
 
-    unroll = 16
+    unroll = 64
 
     @pl.loop(0, particles // unroll)
     def _(step):
@@ -351,9 +360,14 @@
     row_total = jnp.sum(row_sum, axis=1, keepdims=True)
     logz = row_top + jnp.log(row_total)
     for half in range(orients):
-        rounded = (shifted[half] / row_total).astype(BF16).astype(F32)
-        outgoing[half] = jnp.where(lane == owned, logz, rounded)
+        rounded = (shifted[half] / row_total).astype(BF16)
+        outgoing[half] = rounded.astype(outgoing.dtype)
+    own_slot = orient * shells + shell
+    logz_ref[own_slot] = jnp.broadcast_to(logz, logz_ref.shape[1:])
     each(lambda peer: weight_copy(peer, me).start())
+    in_dom = near(dom, True)
+    for peer in in_dom:
+        logz_copy(peer, own_slot).start()
     weights_ref[me] = outgoing[orient]
     out_copy.wait()
 
@@ -363,6 +377,10 @@
 
     each(lambda peer: weight_copy(peer, number(peer)).wait_recv())
     each(finish)
+    for peer in in_dom:
+        logz_copy(peer, peer[1] * shells + peer[2]).wait_recv()
+    for peer in in_dom:
+        logz_copy(peer, own_slot).wait_send()
 
 
 def assign(particle_tile, particle_offset, wedge_slope, tiles, rot_ref, peers):
@@ -394,18 +412,20 @@
     y_table = np.stack(y_table, axis=1)
     particles = particle_tile.shape[0]
     owned, depth = rot_ref.shape
-    width = round_up(owned + 1, LANES)
+    width = round_up(owned, LANES)
     blocks = (count, particles // count, width)
     dma = pltpu.SemaphoreType.DMA
-    weighted, weights, hot = pl.pallas_call(
+    kind = BF16 if blocks[1] % 16 == 0 else F32
+    weighted, weights, logz, hot = pl.pallas_call(
         functools.partial(assign_kernel, peers, sub_rows, owned),
         out_shape=(
             jax.ShapeDtypeStruct((particles, depth), BF16),
-            jax.ShapeDtypeStruct(blocks, F32),
+            jax.ShapeDtypeStruct(blocks, kind),
+            jax.ShapeDtypeStruct((orients * shells, blocks[1], LANES), F32),
             jax.ShapeDtypeStruct((particles, LANES), BF16),
         ),
         in_specs=[SMEM, SMEM, SMEM, VMEM, VMEM, ANY, ANY],
-        out_specs=(ANY, VMEM, VMEM),
+        out_specs=(ANY, VMEM, VMEM, VMEM),
         scratch_shapes=[
             pltpu.VMEM(y_table.shape, BF16),
             pltpu.VMEM(rot_ref.shape, BF16),
@@ -419,7 +439,7 @@
             pltpu.VMEM((particles, LANES), jnp.int32),
             pltpu.VMEM(blocks, F32),
             pltpu.VMEM(blocks, F32),
-            pltpu.VMEM((orients,) + blocks[1:], F32),
+            pltpu.VMEM((orients,) + blocks[1:], kind),
             dma((doms,)),
             dma((doms,)),
             dma((doms, orients)),
@@ -430,28 +450,24 @@
             dma((count,)),
             dma((count,)),
             dma((count,)),
+            dma((orients * shells,)),
+            dma((orients * shells,)),
         ],
         compiler_params=pltpu.CompilerParams(
             collective_id=0, has_side_effects=True, vmem_limit_bytes=LIMIT
         ),
         name="assign",
     )(particle_tile, particle_offset.T, wedge_slope, tiles.reshape(tile_dev * side, side), x_table, y_table, rot_ref)
-    return weighted, weights.reshape(particles, width), hot
+    return weighted, weights.reshape(particles, width), logz.reshape(-1, LANES), hot
 
 
 def average_kernel(
-    sub_rows, shells, owned, slope_ref, weights_ref, weighted_ref, hot_ref, out_ref, logz_ref
+    sub_rows, shells, owned, slope_ref, weights_ref, rows_ref, weighted_ref, hot_ref, out_ref, logz_ref
 ):
     dom = lax.axis_index("dom")
     position = dom * shells + lax.axis_index("shell")
-    turned = weights_ref[...].T
-    part_dev = logz_ref.shape[1]
-    particles = turned.shape[1]
-    logz_row = jnp.broadcast_to(turned[owned : owned + 1], (8, particles))
-    logz_ref[...] = pltpu.roll(logz_row, lax.rem(particles - dom * part_dev, particles), 1)[
-        :1, :part_dev
-    ]
-    kept = turned[:owned].astype(BF16)
+    logz_ref[...] = rows_ref[...].T[:1]
+    kept = weights_ref[...].astype(F32).T[:owned].astype(BF16)
     tomo_weight = jnp.dot(kept, hot_ref[...], preferred_element_type=F32)[:, :TOMOS]
     pieces = []
     rest = tomo_weight
@@ -475,7 +491,7 @@
         out_ref[:, span] = numerator / (denominator + 1.0)
 
 
-def average(wedge_slope, weights, weighted, hot, owned, doms, shells):
+def average(wedge_slope, weights, rows, weighted, hot, owned, doms, shells):
     part_dev = weights.shape[0] // doms
     return pl.pallas_call(
         functools.partial(average_kernel, BOX // (doms * shells), shells, owned),
@@ -483,22 +499,22 @@
             jax.ShapeDtypeStruct((owned, weighted.shape[1]), F32),
             jax.ShapeDtypeStruct((1, part_dev), F32),
         ),
-        in_specs=[SMEM, VMEM, VMEM, VMEM],
+        in_specs=[SMEM, VMEM, VMEM, VMEM, VMEM],
         out_specs=(VMEM, VMEM),
         compiler_params=pltpu.CompilerParams(vmem_limit_bytes=LIMIT),
         name="average",
-    )(wedge_slope, weights, weighted, hot)
+    )(wedge_slope, weights, rows, weighted, hot)
 
 
 def local(tiles, particle_tile, particle_offset, wedge_slope, rot_ref):
     doms = lax.axis_size("dom")
     orients = lax.axis_size("orient")
     shells = lax.axis_size("shell")
-    weighted, weights, hot = assign(
+    weighted, weights, rows, hot = assign(
         particle_tile, particle_offset, wedge_slope, tiles, rot_ref, (doms, orients, shells)
     )
     owned = rot_ref.shape[0]
-    new_reference, logz = average(wedge_slope, weights, weighted, hot, owned, doms, shells)
+    new_reference, logz = average(wedge_slope, weights, rows, weighted, hot, owned, doms, shells)
     return new_reference, logz.reshape(-1)
 
 

time: 46.2 us -> 42.6 us (0.922)
  Pallas kernels: 45.4 us -> 41.8 us
    pallas_call x1, Pallas kernels: 42.5 us -> 38.9 us  [assign(): pl.pallas_call(functools.partial(assign_kernel, peers, sub_rows, owned),...]
where the time goes in v4:
time: 42.6 us; the launch traced here: 42.5 us
  Pallas kernels  41.8 us (98%)
  between operations  0.64 us (2%)
    pallas_call x1, Pallas kernels, assign(): pl.pallas_call(functools.partial(assign_kernel, peers, sub_rows, owned),...  38.9 us
    pallas_call x1, Pallas kernels, average(): pl.pallas_call(functools.partial(average_kernel, BOX // (doms * shells),...  2.95 us

profile of v4, /device:TPU:0, one launch (start us, length us, event | category | flops | bytes accessed | tf_op | source)
XLA Modules:
  0.0 42.5 jit_solution(17467747110700535668)
XLA Ops:
  0.6 38.9 %assign.1 = (bf16[256,2304]{1,0:T(8,128)(2,1)}, bf16[16,16,128]{2,1,0:T(8,128)(2,1)}, f32[4,16,128]{2,1,0:T(8,128)}, bf16[256,128]{1,0:T(8,128)(2,1)}) custom-call(s32[256]{0:T(256)} %tile_ref.1, s32[2,256]{1,0:T(2,128)} %bitcast.8, s32[16]{0:T(128)} %slope_ref.3, bf16[1024,128]{1,0:T(8,128)(2,1)} %bitcast.5, f32[8,24,128]{2,1,0:T(8,128)} %constant.4.clone.x_ref, ...), custom_call_target="tpu_custom_call" | custom-call | tf_op jit(solution)/shard_map/assign/pallas_call | solution.py:419
  39.5 3.0 %average.1 = (f32[96,2304]{1,0:T(8,128)}, f32[1,64]{1,0:T(1,128)}) custom-call(s32[16]{0:T(128)} %slope_ref.3, bf16[256,128]{1,0:T(8,128)(2,1)} %bitcast.6, f32[64,128]{1,0:T(8,128)} %bitcast.7, bf16[256,2304]{1,0:T(8,128)(2,1)} %get-tuple-element.10.weighted_ref, bf16[256,128]{1,0:T(8,128)(2,1)} %get-tuple-element.11.hot_ref), custom_call_target="tpu_custom_call" | custom-call | tf_op jit(solution)/shard_map/average/pallas_call | solution.py:496
